TPU v7x, 32 devices: a whole 2x2x4 slice. The times are simulated.
32 devices in a mesh: rep: 2 (over x), grp: 8 (over z, y), loc: 2 (over core).
Axes of the slice: x: 2, y: 2, z: 4, core: 2. Of those that a mesh axis runs over, the one named last changes fastest.
Arguments:
- tokens: bfloat16 [4096, 2048], P(('rep', 'grp', 'loc')), parts along dimension 0, may hold values from -6 to 6
- cotangent: bfloat16 [4096, 2048], P(('rep', 'grp', 'loc')), parts along dimension 0, may hold values from -4 to 4
- expert_ids: int32 [4096, 8], P(('rep', 'grp', 'loc')), parts along dimension 0, may hold values from 0 to 31, as said below
- route_weights: bfloat16 [4096, 8], P(('rep', 'grp', 'loc')), parts along dimension 0, may hold values from 0.049804688 to 0.5
- gate_weight: bfloat16 [32, 2048, 384], P(('grp', 'loc')), may hold values from -0.125 to 0.125
- up_weight: bfloat16 [32, 2048, 384], P(('grp', 'loc')), may hold values from -0.125 to 0.125
- down_weight: bfloat16 [32, 384, 2048], P(('grp', 'loc')), may hold values from -0.3125 to 0.3125
Outputs:
- grad_tokens: bfloat16 [4096, 2048], P(('rep', 'grp', 'loc')), parts along dimension 0
- grad_weights: bfloat16 [4096, 8], P(('rep', 'grp', 'loc')), parts along dimension 0
There are 2 independent parts, one for each index of `rep`. A program takes and returns all parts, laid end to end along the dimension named above; an argument that names none is the same for every part. Nothing has to cross between parts.
Inputs may be any that keep to these rules, and one draw needn't show every extreme that they name: `expert_ids`: each row names 8 distinct experts, two in each of exactly 4 groups (group = id // 4). In each device's aligned block of 128 rows at most 96 rows name any one group, and some groups reach 96 in every block; every expert of a group is named by exactly half of the block's rows that name the group. In all, at most 768 rows name any one expert, and some experts reach it.
All inputs are finite; a program needn't handle non-finite values.
Results may differ from a plain program's by a relative error of at most 0.009.
Values may be sent and summed in bfloat16 or wider, within the bound.
No kernel may reach another device: no remote copies, remote signals or barrier semaphores. Data moves between devices by JAX's collectives and lax.ppermute only.
A program may use at most 128 MiB of HBM per device.

v0:
```python
import jax
import jax.numpy as jnp
from jax import lax
from jax.sharding import PartitionSpec as P

TOP = 8
TOP_GROUPS = 4


def shortened(shard):
    return jax.tree.map(lambda a: a.astype(jnp.bfloat16) if a.dtype == jnp.float32 else a, shard)


def take_rows(values, indices, filler):
    return jnp.take(values, indices, axis=0, mode="fill", fill_value=filler)


def route_table(targets, dest_total, capacity):
    token_total = targets.shape[0]
    dest_iota = jnp.arange(dest_total, dtype=jnp.int32)
    reached = jnp.any(targets[:, :, None] == dest_iota[None, None, :], axis=1)
    ranked = jnp.cumsum(reached.astype(jnp.int32), axis=0) - 1
    slot_of = jnp.where(reached, ranked, capacity)
    dest_grid = jnp.broadcast_to(dest_iota[None, :], slot_of.shape)
    token_grid = jnp.broadcast_to(jnp.arange(token_total, dtype=jnp.int32)[:, None], slot_of.shape)
    sources = jnp.full((dest_total, capacity), token_total, jnp.int32)
    sources = sources.at[dest_grid, slot_of].set(token_grid, mode="drop")
    return (slot_of, sources)


def token_groups(group_ids, group_total):
    token_total = group_ids.shape[0]
    group_iota = jnp.arange(group_total, dtype=jnp.int32)
    reached = jnp.any(group_ids[:, :, None] == group_iota[None, None, :], axis=1)
    ranked = jnp.cumsum(reached.astype(jnp.int32), axis=1) - 1
    column = jnp.where(reached, ranked, TOP_GROUPS)
    token_grid = jnp.broadcast_to(jnp.arange(token_total, dtype=jnp.int32)[:, None], column.shape)
    listed = jnp.full((token_total, TOP_GROUPS), group_total, jnp.int32)
    return listed.at[token_grid, column].set(
        jnp.broadcast_to(group_iota[None, :], column.shape), mode="drop"
    )


def expert_pass(
    token_rows,
    grad_rows,
    id_rows,
    weight_rows,
    gate_weight,
    up_weight,
    down_weight,
    first_expert,
    capacity,
):
    row_total = token_rows.shape[0]
    local_total = gate_weight.shape[0]
    model_width = token_rows.shape[1]
    experts_here = first_expert + jnp.arange(local_total, dtype=jnp.int32)
    matched = id_rows[None, :, :] == experts_here[:, None, None]
    chosen = jnp.any(matched, axis=2)
    weight_of = jnp.sum(
        jnp.where(matched, weight_rows.astype(jnp.float32)[None, :, :], 0.0), axis=2
    )
    ranked = jnp.cumsum(chosen.astype(jnp.int32), axis=1) - 1
    slot_of = jnp.where(chosen, ranked, capacity)
    expert_grid = jnp.broadcast_to(jnp.arange(local_total, dtype=jnp.int32)[:, None], slot_of.shape)
    row_grid = jnp.broadcast_to(jnp.arange(row_total, dtype=jnp.int32)[None, :], slot_of.shape)
    picks = (
        jnp.full((local_total, capacity), row_total, jnp.int32)
        .at[expert_grid, slot_of]
        .set(row_grid, mode="drop")
    )
    buffer_x = take_rows(token_rows, picks, 0)
    buffer_g = take_rows(grad_rows, picks, 0)
    buffer_w = jnp.take_along_axis(weight_of, picks, axis=1, mode="fill", fill_value=0.0)
    gate_act = jnp.einsum("ecd,edf->ecf", buffer_x, gate_weight, preferred_element_type=jnp.float32)
    up_act = jnp.einsum("ecd,edf->ecf", buffer_x, up_weight, preferred_element_type=jnp.float32)
    back_grad = jnp.einsum(
        "ecd,efd->ecf", buffer_g, down_weight, preferred_element_type=jnp.float32
    )
    sigmoid_val = jax.nn.sigmoid(gate_act)
    silu_val = gate_act * sigmoid_val
    route_grad = jnp.sum(back_grad * silu_val * up_act, axis=2)
    hidden_grad = buffer_w[:, :, None] * back_grad
    gate_grad = (
        hidden_grad * up_act * sigmoid_val * (1.0 + gate_act * (1.0 - sigmoid_val))
    ).astype(jnp.bfloat16)
    up_grad = (hidden_grad * silu_val).astype(jnp.bfloat16)
    input_grad = jnp.einsum(
        "ecf,edf->ecd", gate_grad, gate_weight, preferred_element_type=jnp.float32
    )
    input_grad = input_grad + jnp.einsum(
        "ecf,edf->ecd", up_grad, up_weight, preferred_element_type=jnp.float32
    )
    partial_value = jnp.zeros((row_total, model_width), jnp.float32)
    partial_value = partial_value.at[picks.reshape(-1)].add(
        input_grad.reshape(-1, model_width), mode="drop"
    )
    cap_grid = jnp.broadcast_to(jnp.arange(local_total, dtype=jnp.int32)[:, None], picks.shape)
    route_per = (
        jnp.zeros((local_total, row_total), jnp.float32)
        .at[cap_grid, picks]
        .add(route_grad, mode="drop")
    )
    route_rows = jnp.sum(jnp.where(matched, route_per[:, :, None], 0.0), axis=0)
    return (partial_value, route_rows)


def body(tokens, cotangent, expert_ids, route_weights, gate_weight, up_weight, down_weight):
    group_total = lax.axis_size("grp")
    loc_total = lax.axis_size("loc")
    token_total = tokens.shape[0]
    model_width = tokens.shape[1]
    per_device = gate_weight.shape[0]
    per_group = per_device * loc_total
    group_cap = 6 * token_total // group_total
    expert_cap = 3 * token_total * loc_total
    device_rank = lax.axis_index("grp") * loc_total + lax.axis_index("loc")
    first_expert = device_rank * per_device
    group_ids = expert_ids // per_group
    listed = token_groups(group_ids, group_total)
    slot_range = jnp.arange(TOP, dtype=jnp.int32)[None, :]
    slot_of, sources = route_table(group_ids, group_total, group_cap)
    send_x = take_rows(tokens, sources, 0)
    send_g = take_rows(cotangent, sources, 0)
    send_ids = take_rows(expert_ids, sources, -1)
    send_w = take_rows(route_weights, sources, 0)
    recv_x, recv_g, recv_ids, recv_w = (
        lax.all_to_all(send_x, "grp", split_axis=0, concat_axis=0, tiled=True),
        lax.all_to_all(send_g, "grp", split_axis=0, concat_axis=0, tiled=True),
        lax.all_to_all(send_ids, "grp", split_axis=0, concat_axis=0, tiled=True),
        lax.all_to_all(send_w, "grp", split_axis=0, concat_axis=0, tiled=True),
    )
    row_total = group_total * group_cap
    shared_x, shared_g, shared_ids, shared_w = (
        lax.all_gather(recv_x.reshape(row_total, model_width), "loc", axis=0, tiled=True),
        lax.all_gather(recv_g.reshape(row_total, model_width), "loc", axis=0, tiled=True),
        lax.all_gather(shortened(recv_ids.reshape(row_total, TOP)), "loc", axis=0, tiled=True),
        lax.all_gather(recv_w.reshape(row_total, TOP), "loc", axis=0, tiled=True),
    )
    partial_value, route_rows = expert_pass(
        shared_x,
        shared_g,
        shared_ids,
        shared_w,
        gate_weight,
        up_weight,
        down_weight,
        first_expert,
        expert_cap,
    )
    summed, route_sum = (
        lax.psum_scatter(partial_value, "loc", scatter_dimension=0, tiled=True),
        lax.psum_scatter(route_rows, "loc", scatter_dimension=0, tiled=True),
    )
    group_part = summed.astype(jnp.bfloat16).reshape(group_total, group_cap, model_width)
    route_part = route_sum.astype(jnp.bfloat16).reshape(group_total, group_cap, TOP)
    back_terms, back_route = (
        lax.all_to_all(group_part, "grp", split_axis=0, concat_axis=0, tiled=True),
        lax.all_to_all(route_part, "grp", split_axis=0, concat_axis=0, tiled=True),
    )
    slot_pad = jnp.concatenate([slot_of, jnp.full((token_total, 1), group_cap, jnp.int32)], axis=1)
    found = jnp.take_along_axis(slot_pad, listed, axis=1)
    position = jnp.where(found < group_cap, listed * group_cap + found, row_total)
    pieces = take_rows(back_terms.reshape(row_total, model_width), position, 0)
    grad_tokens = jnp.sum(pieces.astype(jnp.float32), axis=1).astype(jnp.bfloat16)
    slot_found = jnp.take_along_axis(slot_of, group_ids, axis=1)
    route_index = (group_ids * group_cap + slot_found) * TOP + slot_range
    grad_weights = back_route.reshape(row_total * TOP)[route_index]
    return (grad_tokens, grad_weights)


def solution(mesh):
    placed = (
        P(("rep", "grp", "loc"), None),
        P(("rep", "grp", "loc"), None),
        P(("rep", "grp", "loc"), None),
        P(("rep", "grp", "loc"), None),
        P(("grp", "loc"), None, None),
        P(("grp", "loc"), None, None),
        P(("grp", "loc"), None, None),
    )
    return jax.shard_map(
        body,
        mesh=mesh,
        in_specs=placed,
        out_specs=(P(("rep", "grp", "loc"), None), P(("rep", "grp", "loc"), None)),
        check_vma=False,
    )
```

profile of v0, /device:TPU:0, one launch (start us, length us, event | category | flops | bytes accessed | tf_op | source)
XLA Modules:
  0.0 492.4 jit_solution(3578897325285133614)
XLA Ops:
  7.2 0.9 copy.108
  8.9 0.7 compare_select_fusion.3
  9.6 0.8 and_reduce_fusion.2
  10.4 0.7 multiply_reduce_fusion.3
  11.5 4.3 scatter_custom_fusion.2
  16.0 8.2 %gather_fusion.9 = bf16[768,2048]{1,0:T(8,128)(2,1)} fusion(bf16[128,2048]{1,0:T(8,128)(2,1)} %param.11, s32[1024]{0:T(1024)S(1)} %pad_clamp_fusion.2), kind=kCustom, calls=%fused_computation.2.clone | custom fusion | bytes 6294528 | tf_op jit(solution)/shard_map/jit(_take)/gather | solution.py:15
  24.3 8.2 %gather_fusion.7 = bf16[768,2048]{1,0:T(8,128)(2,1)} fusion(bf16[128,2048]{1,0:T(8,128)(2,1)} %param.12, s32[1024]{0:T(1024)S(1)} %pad_clamp_fusion.2), kind=kCustom, calls=%fused_computation.clone | custom fusion | bytes 6294528 | tf_op jit(solution)/shard_map/jit(_take)/gather | solution.py:15
  32.5 4.3 broadcast_select_fusion.4
  36.8 77.9 %all_to_all.30 = bf16[8,96,2048]{2,1,0:T(8,128)(2,1)} all-to-all(bf16[8,96,2048]{2,1,0:T(8,128)(2,1)S(1)} %get-tuple-element.22), channel_id=1, replica_groups=mesh['rep'=2,'grp'=8,'loc'=2] {'grp'}, dimensions={0} | all-to-all | bytes 6291456 | tf_op jit(solution)/shard_map/all_to_all | solution.py:130
  114.8 74.4 %all_to_all.31 = bf16[8,96,2048]{2,1,0:T(8,128)(2,1)} all-to-all(bf16[8,96,2048]{2,1,0:T(8,128)(2,1)} %get-tuple-element.23), channel_id=1, replica_groups=mesh['rep'=2,'grp'=8,'loc'=2] {'grp'}, dimensions={0} | all-to-all | bytes 6291456 | tf_op jit(solution)/shard_map/all_to_all | solution.py:129
  189.2 0.7 copy-done.8
  190.0 1.9 gather_fusion.1
  192.6 3.4 all-to-all-start.1
  196.1 2.3 gather_fusion
  198.4 1.2 copy.126
  199.6 0.6 broadcast_select_fusion.7
  200.2 2.4 all-to-all-done.1
  202.7 3.6 all-to-all-start
  206.4 1.8 all_gather.13
  208.3 4.7 all-to-all-done
  213.0 1.8 all_gather.12
  216.3 11.8 %scatter_custom_fusion.3 = s32[1536]{0:T(1024)S(1)} fusion(s32[3072]{0:T(1024)S(1)} %reshape.402, s32[3072]{0:T(1024)S(1)} %reshape.404, s32[]{:T(128)} %constant.130.clone.1), kind=kCustom, calls=%fused_computation.96 | custom fusion | bytes 6148
  228.5 16.6 %gather_fusion.8 = bf16[1536,2048]{1,0:T(8,128)(2,1)} fusion(bf16[1536,2048]{1,0:T(8,128)(2,1)} %all-gather.3.cloned.1.call-done, s32[2048]{0:T(1024)S(1)} %pad_clamp_fusion), kind=kCustom, calls=%fused_computation.1.clone | custom fusion | bytes 12589056 | tf_op jit(solution)/shard_map/jit(_take)/gather | solution.py:15
  245.1 7.9 %fusion = f32[2,768,384]{1,2,0:T(8,128)} fusion(bf16[2,384,2048]{2,1,0:T(8,128)(2,1)} %param.17, bf16[2,768,2048]{2,1,0:T(8,128)(2,1)} %bitcast.74, pred[2,768]{1,0:T(4,128)(4,1)S(1)} %compare_and_fusion), kind=kOutput, calls=%fused_computation.16 | convolution fusion | flops 2419064832 | bytes 11798016 | tf_op jit(solution)/shard_map/ecd,efd->ecf/dot_general | solution.py:78
  253.0 16.3 %gather_fusion.10 = bf16[1536,2048]{1,0:T(8,128)(2,1)} fusion(bf16[1536,2048]{1,0:T(8,128)(2,1)} %all-gather.5.cloned.1.call-done, s32[2048]{0:T(1024)S(1)} %pad_clamp_fusion), kind=kCustom, calls=%fused_computation.3.clone | custom fusion | bytes 12589056 | tf_op jit(solution)/shard_map/jit(_take)/gather | solution.py:15
  269.3 6.8 %fusion.5 = f32[2,768,384]{1,2,0:T(8,128)S(1)} fusion(bf16[2,2048,384]{2,1,0:T(8,128)(2,1)} %param.15, bf16[2,768,2048]{2,1,0:T(8,128)(2,1)} %bitcast.72, pred[2,768]{1,0:T(4,128)(4,1)S(1)} %compare_and_fusion), kind=kOutput, calls=%fused_computation.22 | convolution fusion | flops 2419064832 | bytes 11798016 | tf_op jit(solution)/shard_map/ecd,edf->ecf/dot_general | solution.py:76
  276.1 5.4 %multiply_reduce_fusion = (f32[2,768]{1,0:T(2,128)S(1)}, f32[2,768,384]{1,2,0:T(8,128)}) fusion(f32[2,768,384]{1,2,0:T(8,128)S(1)} %copy-done.2, f32[2,768,384]{1,2,0:T(8,128)S(1)} %fusion.5, bf16[2,2048,384]{2,1,0:T(8,128)(2,1)S(1)} %copy-done, bf16[2,768,2048]{2,1,0:T(8,128)(2,1)S(1)} %bitcast.73, pred[2,768]{1,0:T(4,128)(4,1)S(1)} %compare_and_fusion), kind=kOutput, calls=%fused_computation.30 | convolution fusion | flops 2423192064 | bytes 16522752 | tf_op jit(solution)/shard_map/ecd,edf->ecf/dot_general | solution.py:77
  281.5 22.1 %scatter_custom_fusion.4 = f32[3072]{0:T(1024)S(1)} fusion(s32[1536]{0:T(1024)S(1)} %reshape.408, f32[1536]{0:T(1024)S(1)} %reshape.410, f32[]{:T(128)} %constant.129.clone.1), kind=kCustom, calls=%fused_computation.89 | custom fusion | flops 1536 | bytes 12292
  303.6 0.7 fusion.17
  304.3 13.4 %gather_fusion.5 = f32[1536]{0:T(1024)S(1)} fusion(f32[2,1536]{1,0:T(2,128)S(1)} %get-tuple-element.15, s32[1536]{0:T(1024)S(1)} %reshape.370), kind=kCustom, calls=%fused_computation.9 | custom fusion | bytes 24576 | tf_op jit(solution)/shard_map/jit(take_along_axis)/gather | solution.py:75
  317.8 12.9 %fusion.11 = f32[2,768,2048]{2,1,0:T(8,128)} fusion(bf16[2,2048,384]{2,1,0:T(8,128)(2,1)} %param.15, f32[2,768,384]{1,2,0:T(8,128)} %copy-done.4, f32[2,768,384]{1,2,0:T(8,128)} %get-tuple-element.25, f32[2,768,384]{1,2,0:T(8,128)} %fusion, f32[2,768]{1,0:T(2,128)S(1)} %broadcast_select_fusion.11), kind=kOutput, calls=%fused_computation.36 | convolution fusion | flops 2422407168 | bytes 22812672 | tf_op jit(solution)/shard_map/ecf,edf->ecd/dot_general | solution.py:89
  330.7 9.9 %convolution_add_fusion = f32[2,768,2048]{2,1,0:T(8,128)} fusion(f32[2,768,2048]{2,1,0:T(8,128)} %fusion.11, bf16[2,2048,384]{2,1,0:T(8,128)(2,1)S(1)} %copy-done, f32[2,768,384]{1,2,0:T(8,128)S(1)} %copy-done.3, f32[2,768]{1,0:T(2,128)S(1)} %broadcast_select_fusion.11, f32[2,768,384]{1,2,0:T(8,128)S(1)} %copy-done.5), kind=kOutput, calls=%fused_computation.24 | convolution fusion | flops 2423193600 | bytes 33036288 | tf_op jit(solution)/shard_map/ecf,edf->ecd/dot_general | solution.py:92
  340.6 26.1 %scatter_custom_fusion = f32[1536,2048]{1,0:T(8,128)} fusion(s32[1536]{0:T(1024)S(1)} %fusion.21, f32[1536,2048]{1,0:T(8,128)} %bitcast.67, f32[]{:T(128)} %constant.129.clone.1), kind=kCustom, calls=%fused_computation.18 | custom fusion | flops 3145728 | bytes 12583424 | tf_op jit(solution)/shard_map/scatter-add | solution.py:96
  366.8 0.7 convert_element_type.43
  367.6 0.6 copy.136
  368.2 3.3 all-to-all-start.5
  371.6 15.2 %reduce-scatter.3.cloned.1.call-done = f32[768,2048]{1,0:T(8,128)} async-done(((f32[1536,2048]{1,0:T(8,128)}), f32[768,2048]{1,0:T(8,128)}) %reduce-scatter.3.cloned.1.call-update) | async-done | bytes 6291472 | tf_op jit(solution)/shard_map/reduce_scatter | solution.py:153
  386.8 5.0 %convert_element_type.42 = bf16[768,2048]{1,0:T(8,128)(2,1)} convert(f32[768,2048]{1,0:T(8,128)} %reduce-scatter.3.cloned.1.call-done) | non-fusion elementwise | flops 1572864 | bytes 9437184 | tf_op jit(solution)/shard_map/convert_element_type | solution.py:156
  391.8 6.0 %all-to-all-start.4 = ((bf16[8,96,2048]{2,1,0:T(8,128)(2,1)}), bf16[8,96,2048]{2,1,0:T(8,128)(2,1)}, u32[]{:S(2)}, u32[]{:S(2)}) async-start(bf16[8,96,2048]{2,1,0:T(8,128)(2,1)} %bitcast.17), calls=%async_computation.5 | async-start | bytes 6291456 | tf_op jit(solution)/shard_map/all_to_all | solution.py:159
  398.0 7.1 %gather_fusion.6 = s32[1024]{0:T(1024)S(1)} fusion(s32[128,8]{1,0:T(8,128)S(1)} %add_select_fusion.1, s32[1024]{0:T(1024)S(1)} %reshape.376), kind=kCustom, calls=%fused_computation.10 | custom fusion | bytes 16384 | tf_op jit(solution)/shard_map/jit(take_along_axis)/gather | solution.py:167
  406.1 4.3 scatter_custom_fusion.1
  410.6 3.8 gather_fusion.4
  415.3 6.8 %gather_fusion.3 = bf16[1024]{0:T(1024)(128)(2,1)S(1)} fusion(bf16[6144]{0:T(1024)(128)(2,1)S(1)} %reshape.280, s32[1024]{0:T(1024)S(1)} %broadcast_clamp_fusion), kind=kCustom, calls=%fused_computation.7 | custom fusion | bytes 8192 | tf_op jit(solution)/shard_map/gather | solution.py:169
  422.2 0.7 copy.138
  422.9 46.1 %all-to-all-done.4 = bf16[8,96,2048]{2,1,0:T(8,128)(2,1)} async-done(((bf16[8,96,2048]{2,1,0:T(8,128)(2,1)}), bf16[8,96,2048]{2,1,0:T(8,128)(2,1)}, u32[]{:S(2)}, u32[]{:S(2)}) %all-to-all-start.4) | async-done | bytes 3145760 | tf_op jit(solution)/shard_map/all_to_all | solution.py:159
  469.0 7.7 %gather_fusion.2 = bf16[512,2048]{1,0:T(8,128)(2,1)} fusion(bf16[768,2048]{1,0:T(8,128)(2,1)} %bitcast.18, s32[1024]{0:T(1024)S(1)} %pad_clamp_fusion.1), kind=kCustom, calls=%fused_computation.6 | custom fusion | bytes 4196352 | tf_op jit(solution)/shard_map/jit(_take)/gather | solution.py:15
  476.7 4.1 reshape.349
  480.8 4.6 select_reduce_fusion
  (137 shorter events, 6.9 us)
Async XLA Ops:
  7.2 268.9 %copy-start = (bf16[2,2048,384]{2,1,0:T(8,128)(2,1)S(1)}, bf16[2,2048,384]{2,1,0:T(8,128)(2,1)}, u32[]{:S(2)}) copy-start(bf16[2,2048,384]{2,1,0:T(8,128)(2,1)} %param.16) | copy-start | bytes 9437188
  7.2 221.3 %all-gather.3.cloned.1.call-start = ((), (), s32[]{:S(2)}) async-start(), calls=%async_computation.8 | async-start | bytes 9437184 | tf_op jit(solution)/shard_map/all_gather | solution.py:137
  114.7 138.3 %all-gather.5.cloned.1.call-start = ((), (), s32[]{:S(2)}) async-start(), calls=%async_computation.9 | async-start | bytes 9437184 | tf_op jit(solution)/shard_map/all_gather | solution.py:136
  189.2 0.7 copy-start.8
  190.0 26.1 %copy-start.10 = (s32[2]{0:T(128)S(1)}, s32[2]{0:T(128)}, u32[]{:S(2)}) copy-start(s32[2]{0:T(128)} %constant.195) | copy-start | bytes 28
  190.0 26.2 %copy-start.9 = (s32[2]{0:T(128)S(1)}, s32[2]{0:T(128)}, u32[]{:S(2)}) copy-start(s32[2]{0:T(128)} %constant.198) | copy-start | bytes 28
  190.0 38.2 %copy-start.14 = (s32[2]{0:T(128)S(1)}, s32[2]{0:T(128)}, u32[]{:S(2)}) copy-start(s32[2]{0:T(128)} %constant.201) | copy-start | bytes 28
  190.0 38.3 %copy-start.13 = (s32[2]{0:T(128)S(1)}, s32[2]{0:T(128)}, u32[]{:S(2)}) copy-start(s32[2]{0:T(128)} %constant.204) | copy-start | bytes 28
  192.6 10.0 %all-to-all-start.1 = ((bf16[8,96,8]{1,2,0:T(8,128)(2,1)}), bf16[8,96,8]{1,2,0:T(8,128)(2,1)S(1)}, u32[]{:S(2)}, u32[]{:S(2)}) async-start(bf16[8,96,8]{1,2,0:T(8,128)(2,1)} %broadcast_select_fusion.8), calls=%async_computation.1 | async-start | bytes 32768 | tf_op jit(solution)/shard_map/all_to_all | solution.py:132
  202.7 10.3 %all-to-all-start = ((s32[8,96,8]{1,2,0:T(8,128)}), s32[8,96,8]{1,2,0:T(8,128)S(1)}, u32[]{:S(2)}, u32[]{:S(2)}) async-start(s32[8,96,8]{1,2,0:T(8,128)} %broadcast_select_fusion.7), calls=%async_computation | async-start | bytes 65536 | tf_op jit(solution)/shard_map/all_to_all | solution.py:131
  206.2 160.5 %reduce-scatter.5.cloned.1.call-start = ((), (), s32[]{:S(2)}) async-start(), calls=%async_computation.11 | async-start | bytes 73728 | tf_op jit(solution)/shard_map/reduce_scatter | solution.py:154
  269.3 6.8 %copy-start.2 = (f32[2,768,384]{1,2,0:T(8,128)S(1)}, f32[2,768,384]{1,2,0:T(8,128)}, u32[]{:S(2)}) copy-start(f32[2,768,384]{1,2,0:T(8,128)} %fusion) | copy-start | bytes 7077892
  269.3 6.8 %copy-start.6 = (bf16[1536,2048]{1,0:T(8,128)(2,1)S(1)}, bf16[1536,2048]{1,0:T(8,128)(2,1)}, u32[]{:S(2)}) copy-start(bf16[1536,2048]{1,0:T(8,128)(2,1)} %gather_fusion.10) | copy-start | bytes 18874372
  276.1 5.4 %copy-start.4 = (f32[2,768,384]{1,2,0:T(8,128)}, f32[2,768,384]{1,2,0:T(8,128)S(1)}, u32[]{:S(2)}) copy-start(f32[2,768,384]{1,2,0:T(8,128)S(1)} %fusion.5) | copy-start | bytes 7077892
  317.8 69.1 %reduce-scatter.3.cloned.1.call-start = ((), (), s32[]{:S(2)}) async-start(), calls=%async_computation.10 | async-start | bytes 18874368 | tf_op jit(solution)/shard_map/reduce_scatter | solution.py:153
  317.8 12.9 %copy-start.3 = (f32[2,768,384]{1,2,0:T(8,128)S(1)}, f32[2,768,384]{1,2,0:T(8,128)}, u32[]{:S(2)}) copy-start(f32[2,768,384]{1,2,0:T(8,128)} %fusion) | copy-start | bytes 7077892
  317.8 12.9 %copy-start.5 = (f32[2,768,384]{1,2,0:T(8,128)S(1)}, f32[2,768,384]{1,2,0:T(8,128)}, u32[]{:S(2)}) copy-start(f32[2,768,384]{1,2,0:T(8,128)} %copy-done.4) | copy-start | bytes 7077892
  368.2 23.5 %all-to-all-start.5 = ((bf16[8,96,8]{1,2,0:T(8,128)(2,1)}), bf16[8,96,8]{1,2,0:T(8,128)(2,1)S(1)}, u32[]{:S(2)}, u32[]{:S(2)}) async-start(bf16[8,96,8]{1,2,0:T(8,128)(2,1)} %copy.136), calls=%async_computation.7 | async-start | bytes 32768 | tf_op jit(solution)/shard_map/all_to_all | solution.py:160
  391.8 77.2 %all-to-all-start.4 = ((bf16[8,96,2048]{2,1,0:T(8,128)(2,1)}), bf16[8,96,2048]{2,1,0:T(8,128)(2,1)}, u32[]{:S(2)}, u32[]{:S(2)}) async-start(bf16[8,96,2048]{2,1,0:T(8,128)(2,1)} %bitcast.17), calls=%async_computation.5 | async-start | bytes 6291456 | tf_op jit(solution)/shard_map/all_to_all | solution.py:159
  398.0 7.4 %copy-start.7 = (s32[128,8,1]{1,0,2:T(8,128)S(1)}, s32[128,8,1]{1,0,2:T(8,128)}, u32[]{:S(2)}) copy-start(s32[128,8,1]{1,0,2:T(8,128)} %get-tuple-element.18) | copy-start | bytes 12292
  398.0 7.4 %copy-start.12 = (s32[2]{0:T(128)S(1)}, s32[2]{0:T(128)}, u32[]{:S(2)}) copy-start(s32[2]{0:T(128)} %constant.186) | copy-start | bytes 28
  398.0 7.7 %copy-start.11 = (s32[2]{0:T(128)S(1)}, s32[2]{0:T(128)}, u32[]{:S(2)}) copy-start(s32[2]{0:T(128)} %constant.183) | copy-start | bytes 28
  469.0 16.4 %copy-start.1 = (bf16[2,2048,384]{2,1,0:T(8,128)(2,1)S(1)}, bf16[2,2048,384]{2,1,0:T(8,128)(2,1)}, u32[]{:S(2)}) copy-start(bf16[2,2048,384]{2,1,0:T(8,128)(2,1)} %param.16) | copy-start | bytes 9437188
Sparse Core Ops, SparseCore 0:
  114.8 15.7 all-gather.2
  189.3 15.6 all-gather.4
  317.9 5.8 reduce-scatter.4
  366.9 19.8 reduce-scatter.2
where the time goes:
time: 501 us; the launch traced here: 492 us
  blocking collectives  156 us (31%)
  local copies, waits for them, and re-layouts  125 us (25%)
  other arithmetic  69.3 us (14%)
  waiting for transfers between devices  68.5 us (14%)
  matrix products  42.8 us (9%)
  starting transfers between devices  16.5 us (3%)
  between operations  14.8 us (3%)
    all_to_all x1, blocking collectives, body(): lax.all_to_all(send_g, 'grp', split_axis=0, concat_axis=0, tiled=True)  77.9 us
    all_to_all x1, blocking collectives, body(): lax.all_to_all(send_x, 'grp', split_axis=0, concat_axis=0, tiled=True)  74.4 us
    gather x10, local copies, waits for them, and re-layouts, take_rows(): return jnp.take(values, indices, axis=0, mode='fill', fill_value=filler)  66.6 us
    all_to_all x1, waiting for transfers between devices, body(): lax.all_to_all(group_part, 'grp', split_axis=0, concat_axis=0, tiled=True)  46.1 us
    scatter-add x1, other arithmetic, expert_pass(): partial_value.at[picks.reshape(-1)]  26.1 us
    unnamed x13, other arithmetic  24.1 us
    unnamed x44, local copies, waits for them, and re-layouts  23.5 us
    reduce_scatter x1, waiting for transfers between devices, body(): lax.psum_scatter(partial_value, 'loc', scatter_dimension=0, tiled=True)  15.2 us
  transfers between devices with their start and end apart: 8, of which 4 were waited for; matrix products, arithmetic and copies ran while one was open for 25% of the time, Pallas kernels for 0%

commit v1 on v0

--- a/solution.py
+++ b/solution.py
@@ -1,6 +1,10 @@
+import functools
+
 import jax
 import jax.numpy as jnp
 from jax import lax
+from jax.experimental import pallas as pl
+from jax.experimental.pallas import tpu as pltpu
 from jax.sharding import PartitionSpec as P
 
 TOP = 8
@@ -106,7 +110,7 @@
     return (partial_value, route_rows)
 
 
-def body(tokens, cotangent, expert_ids, route_weights, gate_weight, up_weight, down_weight):
+def routed_body(tokens, cotangent, expert_ids, route_weights, gate_weight, up_weight, down_weight):
     group_total = lax.axis_size("grp")
     loc_total = lax.axis_size("loc")
     token_total = tokens.shape[0]
@@ -170,6 +174,184 @@
     return (grad_tokens, grad_weights)
 
 
+LANES = 128
+NT = (((1,), (1,)), ((), ()))
+
+
+def experts_kernel(piece_rows, per_device, place, *refs):
+    pieces = len(piece_rows)
+    x_in, g_in = refs[:pieces], refs[pieces : 2 * pieces]
+    (w_in, gate_own, up_own, down_own, gate_other, up_other, down_other, out, x, g, gate_up, down, total, sems, row_sems) = refs[
+        2 * pieces :
+    ]
+    width = x.shape[1]
+    hidden = down.shape[1]
+    copies = []
+    start = 0
+    for i, rows in enumerate(piece_rows):
+        copies.append(pltpu.make_async_copy(x_in[i], x.at[pl.ds(start, rows)], row_sems.at[0, i]))
+        copies.append(pltpu.make_async_copy(g_in[i], g.at[pl.ds(start, rows)], row_sems.at[1, i]))
+        start += rows
+    for copy in copies:
+        copy.start()
+
+    def weight_copies(e, gate, up, down_weight, source):
+        return (
+            pltpu.make_async_copy(gate.at[source], gate_up.at[e, :, pl.ds(0, hidden)], sems.at[0, e]),
+            pltpu.make_async_copy(up.at[source], gate_up.at[e, :, pl.ds(hidden, hidden)], sems.at[1, e]),
+            pltpu.make_async_copy(down_weight.at[source], down.at[e], sems.at[2, e]),
+        )
+
+    for e in range(2 * per_device):
+        mine = (gate_own, up_own, down_own) if e < per_device else (gate_other, up_other, down_other)
+        for copy in weight_copies(e, *mine, e % per_device):
+            copy.start()
+    for copy in copies:
+        copy.wait()
+    weight_rows = jnp.concatenate(
+        [w_in[pl.ds(pl.multiple_of(place[2 + i], 16), rows), :] for i, rows in enumerate(piece_rows)], axis=0
+    ).astype(jnp.float32)
+    lane = lax.broadcasted_iota(jnp.int32, weight_rows.shape, 1)
+
+    def step(e, route):
+        for copy in weight_copies(e, gate_own, up_own, down_own, 0):
+            copy.wait()
+        column = place[0] + lax.rem(place[1] + e, 2 * per_device)
+        weight = jnp.sum(jnp.where(lane == column, weight_rows, 0.0), axis=1, keepdims=True)
+        both = jnp.dot(x[...], gate_up[e], preferred_element_type=jnp.float32)
+        gate_act, up_act = both[:, :hidden], both[:, hidden:]
+        back = lax.dot_general(g[...], down[e], NT, preferred_element_type=jnp.float32)
+        sig = jax.nn.sigmoid(gate_act)
+        silu = gate_act * sig
+        route_grad = jnp.sum(back * silu * up_act, axis=1, keepdims=True)
+        hidden_grad = weight * back
+        gate_grad = (hidden_grad * up_act * sig * (1.0 + gate_act * (1.0 - sig))).astype(jnp.bfloat16)
+        up_grad = (hidden_grad * silu).astype(jnp.bfloat16)
+        grads = jnp.concatenate([gate_grad, up_grad], axis=1)
+        term = lax.dot_general(grads, gate_up[e], NT, preferred_element_type=jnp.float32)
+
+        @pl.when(e == 0)
+        def _():
+            total[...] = term
+
+        @pl.when(e > 0)
+        def _():
+            total[...] += term
+
+        return route + jnp.where(lane == column, route_grad, 0.0)
+
+    route = lax.fori_loop(0, 2 * per_device, step, jnp.zeros(weight_rows.shape, jnp.float32))
+    out[:, :width] = total[...].astype(out.dtype)
+    out[:, width:] = route.astype(out.dtype)
+
+
+def experts_call(place, xs, gs, weight_table, own, other):
+    piece_rows = tuple(a.shape[0] for a in xs)
+    rows = sum(piece_rows)
+    per_device, width, hidden = own[0].shape
+    anywhere = pl.BlockSpec(memory_space=pl.ANY)
+    return pl.pallas_call(
+        functools.partial(experts_kernel, piece_rows, per_device),
+        out_shape=jax.ShapeDtypeStruct((rows, width + LANES), jnp.bfloat16),
+        in_specs=[pl.BlockSpec(memory_space=pltpu.SMEM)]
+        + [anywhere] * (2 * len(xs))
+        + [pl.BlockSpec(memory_space=pltpu.VMEM)]
+        + [anywhere] * 6,
+        out_specs=pl.BlockSpec(memory_space=pltpu.VMEM),
+        scratch_shapes=[
+            pltpu.VMEM((rows, width), jnp.bfloat16),
+            pltpu.VMEM((rows, width), jnp.bfloat16),
+            pltpu.VMEM((2 * per_device, width, 2 * hidden), jnp.bfloat16),
+            pltpu.VMEM((2 * per_device, hidden, width), jnp.bfloat16),
+            pltpu.VMEM((rows, width), jnp.float32),
+            pltpu.SemaphoreType.DMA((3, 2 * per_device)),
+            pltpu.SemaphoreType.DMA((2, len(xs))),
+        ],
+        compiler_params=pltpu.CompilerParams(vmem_limit_bytes=44 * 1024 * 1024),
+        cost_estimate=pl.CostEstimate(
+            flops=2 * per_device * rows * 10 * width * hidden,
+            bytes_accessed=2 * per_device * 6 * width * hidden + rows * width * 6,
+            transcendentals=2 * per_device * rows * hidden,
+        ),
+    )(place, *xs, *gs, weight_table, *own, *other)
+
+
+def added(a, b):
+    return (a.astype(jnp.float32) + b.astype(jnp.float32)).astype(jnp.bfloat16)
+
+
+def ring_body(tokens, cotangent, expert_ids, route_weights, gate_weight, up_weight, down_weight):
+    ring_total = lax.axis_size("grp")
+    loc_total = lax.axis_size("loc")
+    block, width = tokens.shape
+    per_device = gate_weight.shape[0]
+    expert_total = ring_total * loc_total * per_device
+    order = list(range(0, ring_total, 2)) + list(range(ring_total - 1, 0, -2))
+    ahead = [(order[i], order[(i + 1) % ring_total]) for i in range(ring_total)]
+    behind = [(b, a) for a, b in ahead]
+    rank, loc = lax.axis_index("grp"), lax.axis_index("loc")
+    order_array = jnp.array(order, jnp.int32)
+    position = jnp.argmax(order_array == rank).astype(jnp.int32)
+
+    def send(a, way):
+        return lax.ppermute(a, "grp", way)
+
+    own = (gate_weight, up_weight, down_weight)
+    swap = [(i, loc_total - 1 - i) for i in range(loc_total)]
+    other = tuple(lax.ppermute(a, "loc", swap) for a in own)
+    expert_iota = jnp.arange(LANES, dtype=jnp.int32)
+    named = expert_ids[:, :, None] == expert_iota[None, None, :]
+    table = jnp.sum(jnp.where(named, route_weights.astype(jnp.float32)[:, :, None], 0.0), axis=1)
+    weight_table = lax.all_gather(table.astype(jnp.bfloat16), "grp", axis=0, tiled=True)
+    lane_base = rank * (loc_total * per_device)
+
+    def call(xs, gs, starts):
+        place = jnp.stack([lane_base, loc * per_device] + starts).astype(jnp.int32)
+        return experts_call(place, xs, gs, weight_table, own, other)
+
+    def row_of(distance):
+        return order_array[(position + distance) % ring_total] * block
+
+    half = ring_total // 2
+    cut = block // 2
+    x_up, g_up, x_down, g_down = tokens, cotangent, tokens, cotangent
+    partial_up, partial_down = [None], [None]
+    own_part = call([tokens], [cotangent], [row_of(0)])
+    for s in range(1, half):
+        x_up, x_down = send(x_up, ahead), send(x_down, behind)
+        g_up, g_down = send(g_up, ahead), send(g_down, behind)
+        part = call([x_up, x_down], [g_up, g_down], [row_of(-s), row_of(s)])
+        partial_up.append(part[:block])
+        partial_down.append(part[block:])
+    x_up, x_down = send(x_up[:cut], ahead), send(x_down[cut:], behind)
+    g_up, g_down = send(g_up[:cut], ahead), send(g_down[cut:], behind)
+    part = call([x_up, x_down], [g_up, g_down], [row_of(half), row_of(half) + cut])
+    back_up, back_down = send(part[:cut], behind), send(part[cut:], ahead)
+    for s in range(half - 1, 0, -1):
+        if s == half - 1:
+            mine = partial_up[s]
+            sum_up = jnp.concatenate([added(mine[:cut], back_up), mine[cut:]], axis=0)
+            mine = partial_down[s]
+            sum_down = jnp.concatenate([mine[:cut], added(mine[cut:], back_down)], axis=0)
+        else:
+            sum_up, sum_down = added(partial_up[s], back_up), added(partial_down[s], back_down)
+        back_up, back_down = send(sum_up, behind), send(sum_down, ahead)
+    summed = own_part.astype(jnp.float32) + back_up.astype(jnp.float32) + back_down.astype(jnp.float32)
+    grad_tokens = summed[:, :width].astype(jnp.bfloat16)
+    route = summed[:, width:]
+    grad_weights = jnp.sum(jnp.where(named, route[:, None, :], 0.0), axis=2).astype(jnp.bfloat16)
+    return (grad_tokens, grad_weights)
+
+
+def body(tokens, cotangent, expert_ids, route_weights, gate_weight, up_weight, down_weight):
+    args = (tokens, cotangent, expert_ids, route_weights, gate_weight, up_weight, down_weight)
+    ring_total, loc_total = lax.axis_size("grp"), lax.axis_size("loc")
+    experts = ring_total * loc_total * gate_weight.shape[0]
+    if loc_total == 2 and ring_total % 2 == 0 and 4 <= ring_total <= 8 and experts <= LANES and tokens.shape[0] % 32 == 0:
+        return ring_body(*args)
+    return routed_body(*args)
+
+
 def solution(mesh):
     placed = (
         P(("rep", "grp", "loc"), None),

time: 501 us -> 203 us (0.41); the launches traced: 492 us -> 202 us
  blocking collectives: 156 us -> 30.9 us
  local copies, waits for them, and re-layouts: 125 us -> 11.9 us
  Pallas kernels: 0 us -> 66.1 us
  other arithmetic: 69.3 us -> 3.28 us
  matrix products: 42.8 us -> 0 us
  waiting for transfers between devices: 68.5 us -> 51.2 us
  starting transfers between devices: 16.5 us -> 26.7 us
    all_to_all x2 -> x0, blocking collectives: 152 us -> none  [the longest x1 77.9 us: body(): lax.all_to_all(send_g, 'grp', split_axis=0, concat_axis=0, tiled=True)]
    gather x24 -> x0, local copies, waits for them, and re-layouts: 98.3 us -> none  [the longest x10 66.6 us: take_rows(): return jnp.take(values, indices, axis=0, mode='fill', fill_value=filler)]
    pallas_call x0 -> x5, Pallas kernels: none -> 66.1 us  [experts_call(): pl.pallas_call(functools.partial(experts_kernel, piece_rows, per_device),...]
    all_to_all x4 -> x0, waiting for transfers between devices: 53.2 us -> none  [the longest x1 46.1 us: body(): lax.all_to_all(group_part, 'grp', split_axis=0, concat_axis=0, tiled=True)]
    ppermute x0 -> x27, waiting for transfers between devices: none -> 51.2 us  [the longest x24 51.2 us: send(): return lax.ppermute(a, 'grp', way)]
    dot_general x5 -> x0, matrix products: 42.8 us -> none  [the longest x1 12.9 us: expert_pass(): jnp.einsum('ecf,edf->ecd', gate_grad, gate_weight, preferred_element_type...]
    all_gather x2 -> x1, blocking collectives: 3.64 us -> 30.9 us  [ring_body(): lax.all_gather(table.astype(jnp.bfloat16), 'grp', axis=0, tiled=True)]
    ppermute x0 -> x27, starting transfers between devices: none -> 26.7 us  [the longest x24 26.7 us: send(): return lax.ppermute(a, 'grp', way)]
  transfers between devices with their start and end apart: 8 -> 27, of which waited for: 4 -> 9; matrix products, arithmetic and copies ran while one was open for 25% -> 3% of each run, Pallas kernels for 0% -> 27%
where the time goes in v1:
time: 203 us; the launch traced here: 202 us
  Pallas kernels  66.1 us (33%)
  waiting for transfers between devices  51.2 us (25%)
  blocking collectives  30.9 us (15%)
  starting transfers between devices  26.7 us (13%)
  between operations  12.3 us (6%)
  local copies, waits for them, and re-layouts  11.9 us (6%)
  other arithmetic  3.28 us (2%)
    pallas_call x5, Pallas kernels, experts_call(): pl.pallas_call(functools.partial(experts_kernel, piece_rows, per_device),...  66.1 us
    ppermute x24, waiting for transfers between devices, send(): return lax.ppermute(a, 'grp', way)  51.2 us
    all_gather x1, blocking collectives, ring_body(): lax.all_gather(table.astype(jnp.bfloat16), 'grp', axis=0, tiled=True)  30.9 us
    ppermute x24, starting transfers between devices, send(): return lax.ppermute(a, 'grp', way)  26.7 us
    unnamed x28, local copies, waits for them, and re-layouts  8.46 us
  transfers between devices with their start and end apart: 27, of which 9 were waited for; matrix products, arithmetic and copies ran while one was open for 3% of the time, Pallas kernels for 27%

profile of v1, /device:TPU:0, one launch (start us, length us, event | category | flops | bytes accessed | tf_op | source)
XLA Modules:
  0.0 202.5 jit_solution(11933422882786734345)
XLA Ops:
  0.6 3.1 %collective-permute-start.3 = (bf16[128,2048]{1,0:T(8,128)(2,1)}, bf16[128,2048]{1,0:T(8,128)(2,1)S(1)}, u32[]{:S(2)}, u32[]{:S(2)}) collective-permute-start(bf16[128,2048]{1,0:T(8,128)(2,1)} %refs_0_.1), channel_id=1, source_target_pairs={{0,4},{4,8},{8,12},{12,14},{14,10},{10,6},{6,2},{2,0},{1,5},{5,9},... | collective-permute-start | bytes 1572872 | tf_op jit(solution)/shard_map/ppermute | solution.py:297
  3.7 2.0 collective-permute-start.5
  5.7 10.9 %collective-permute-done.3.refs_0_ = bf16[128,2048]{1,0:T(8,128)(2,1)S(1)} collective-permute-done((bf16[128,2048]{1,0:T(8,128)(2,1)}, bf16[128,2048]{1,0:T(8,128)(2,1)S(1)}, u32[]{:S(2)}, u32[]{:S(2)}) %collective-permute-start.3) | collective-permute-done | bytes 524320 | tf_op jit(solution)/shard_map/ppermute | solution.py:297
  16.6 2.1 %collective-permute-done.4.refs_1_ = bf16[128,2048]{1,0:T(8,128)(2,1)S(1)} collective-permute-done((bf16[128,2048]{1,0:T(8,128)(2,1)}, bf16[128,2048]{1,0:T(8,128)(2,1)S(1)}, u32[]{:S(2)}, u32[]{:S(2)}) %collective-permute-start.4) | collective-permute-done | bytes 524320 | tf_op jit(solution)/shard_map/ppermute | solution.py:297
  18.8 8.3 %collective-permute-done.5.refs_2_ = bf16[128,2048]{1,0:T(8,128)(2,1)S(1)} collective-permute-done((bf16[128,2048]{1,0:T(8,128)(2,1)}, bf16[128,2048]{1,0:T(8,128)(2,1)S(1)}, u32[]{:S(2)}, u32[]{:S(2)}) %collective-permute-start.5) | collective-permute-done | bytes 524320 | tf_op jit(solution)/shard_map/ppermute | solution.py:297
  27.0 1.8 collective-permute-start.7
  29.1 11.1 %collective-permute-done.7.refs_0_ = bf16[128,2048]{1,0:T(8,128)(2,1)S(1)} collective-permute-done((bf16[128,2048]{1,0:T(8,128)(2,1)S(1)}, bf16[128,2048]{1,0:T(8,128)(2,1)S(1)}, u32[]{:S(2)}, u32[]{:S(2)}) %collective-permute-start.7) | collective-permute-done | bytes 524320 | tf_op jit(solution)/shard_map/ppermute | solution.py:297
  40.1 1.5 collective-permute-start.9
  41.6 0.8 copy-done.5
  42.4 0.6 collective-permute-start.10
  43.0 0.8 copy-done.7
  43.8 8.7 %collective-permute-done.9.refs_2_ = bf16[128,2048]{1,0:T(8,128)(2,1)} collective-permute-done((bf16[128,2048]{1,0:T(8,128)(2,1)S(1)}, bf16[128,2048]{1,0:T(8,128)(2,1)}, u32[]{:S(2)}, u32[]{:S(2)}) %collective-permute-start.9) | collective-permute-done | bytes 524320 | tf_op jit(solution)/shard_map/ppermute | solution.py:297
  52.4 1.3 collective-permute-start.11
  53.7 0.8 copy-done.9
  54.5 0.8 collective-permute-start.12
  55.3 0.8 copy-done.11
  56.1 8.2 %collective-permute-done.11.refs_0_ = bf16[128,2048]{1,0:T(8,128)(2,1)S(1)} collective-permute-done((bf16[128,2048]{1,0:T(8,128)(2,1)S(1)}, bf16[128,2048]{1,0:T(8,128)(2,1)S(1)}, u32[]{:S(2)}, u32[]{:S(2)}) %collective-permute-start.11) | collective-permute-done | bytes 524320 | tf_op jit(solution)/shard_map/ppermute | solution.py:297
  64.3 1.3 collective-permute-start.13
  65.6 0.8 collective-permute-done.12.refs_1_
  66.4 0.8 collective-permute-start.14
  67.1 1.3 compare_reduce_fusion
  74.7 1.6 fusion.2
  77.7 0.8 copy.12
  78.5 0.8 copy.13
  79.3 1.3 collective-permute-start.15
  80.6 0.8 collective-permute-start.16
  81.4 0.4 select_reduce_fusion.1
  81.7 30.9 %all_gather.3.refs_2_.refs_4_ = bf16[1024,128]{1,0:T(8,128)(2,1)S(1)} all-gather(bf16[128,128]{1,0:T(8,128)(2,1)S(1)} %select_reduce_fusion.1), channel_id=1, replica_groups=mesh['rep'=2,'grp'=8,'loc'=2] {'grp'}, dimensions={0}, use_global_device_ids=true | all-gather | bytes 294912 | tf_op jit(solution)/shard_map/all_gather | solution.py:305
  112.8 2.0 collective-permute-start.18
  118.1 1.1 collective-permute-done.17.refs_2_
  119.3 1.9 copy-done
  121.1 1.9 copy-done.2
  123.0 11.3 %shard_map.99 = bf16[128,2176]{1,0:T(8,128)(2,1)S(1)} custom-call(s32[4]{0:T(128)S(1)} %get-tuple-element.28.place, bf16[64,2048]{1,0:T(8,128)(2,1)S(1)} %collective-permute-done.15.refs_0_, bf16[64,2048]{1,0:T(8,128)(2,1)S(1)} %collective-permute-done.16.refs_1_, bf16[64,2048]{1,0:T(8,128)(2,1)S(1)} %collective-permute-done.17.refs_2_, ...), custom_call_target="tpu_custom_call" | custom-call | flops 4026531840 | bytes 20447232 | tf_op jit(solution)/shard_map/pallas_call | solution.py:253
  134.4 2.0 collective-permute-start.19
  136.4 14.6 %shard_map.98 = bf16[256,2176]{1,0:T(8,128)(2,1)S(1)} custom-call(s32[4]{0:T(128)S(1)} %get-tuple-element.27.place, bf16[128,2048]{1,0:T(8,128)(2,1)S(1)} %collective-permute-done.11.refs_0_, bf16[128,2048]{1,0:T(8,128)(2,1)S(1)} %collective-permute-done.12.refs_1_, bf16[128,2048]{1,0:T(8,128)(2,1)S(1)} %collective-permute-done.13.refs_2_, ...), custom_call_target="tpu_custom_call" | custom-call | flops 8053063680 | bytes 22020096 | tf_op jit(solution)/shard_map/pallas_call | solution.py:253
  151.3 2.0 collective-permute-start.24
  153.3 0.3 collective-permute-start.20
  153.6 14.6 %shard_map.97 = bf16[256,2176]{1,0:T(8,128)(2,1)S(1)} custom-call(s32[4]{0:T(128)S(1)} %get-tuple-element.26.place, bf16[128,2048]{1,0:T(8,128)(2,1)S(1)} %copy-done.10, bf16[128,2048]{1,0:T(8,128)(2,1)S(1)} %copy-done.12, bf16[128,2048]{1,0:T(8,128)(2,1)} %collective-permute-done.9.refs_2_, bf16[128,2048]{1,0:T(8,128)(2,1)} %collective-permute-done.10.refs_3_, ...), custom_call_target="tpu_custom_call" | custom-call | flops 8053063680 | bytes 22020096 | tf_op jit(solution)/shard_map/pallas_call | solution.py:253
  168.3 0.3 add_convert_fusion.3
  168.5 2.0 collective-permute-start.21
  170.5 0.9 collective-permute-start.25
  171.4 14.6 %shard_map.96 = bf16[256,2176]{1,0:T(8,128)(2,1)S(1)} custom-call(s32[4]{0:T(128)S(1)} %get-tuple-element.6.place, bf16[128,2048]{1,0:T(8,128)(2,1)S(1)} %collective-permute-done.3.refs_0_, bf16[128,2048]{1,0:T(8,128)(2,1)S(1)} %collective-permute-done.4.refs_1_, bf16[128,2048]{1,0:T(8,128)(2,1)S(1)} %copy-done.6, bf16[128,2048]{1,0:T(8,128)(2,1)S(1)} %copy-done.8, ...), custom_call_target="tpu_custom_call" | custom-call | flops 8053063680 | bytes 22020096 | tf_op jit(solution)/shard_map/pallas_call | solution.py:253
  186.3 1.3 collective-permute-start.22
  187.6 0.8 collective-permute-start.26
  189.1 11.2 %shard_map.95 = bf16[128,2176]{1,0:T(8,128)(2,1)S(1)} custom-call(s32[3]{0:T(128)S(1)} %pad_add_fusion.place, bf16[128,2048]{1,0:T(8,128)(2,1)S(1)} %copy-done.3, bf16[128,2048]{1,0:T(8,128)(2,1)S(1)} %copy-done.4, bf16[1024,128]{1,0:T(8,128)(2,1)S(1)} %all_gather.3.refs_2_.refs_4_, bf16[2,2048,384]{2,1,0:T(8,128)(2,1)S(1)} %copy-done.1, ...), custom_call_target="tpu_custom_call" | custom-call | flops 4026531840 | bytes 20447232 | tf_op jit(solution)/shard_map/pallas_call | solution.py:253
  200.5 0.9 slice.94
  201.4 0.4 select_reduce_fusion
  201.8 0.7 copy.14
  (62 shorter events, 1.6 us)
Async XLA Ops:
  0.6 16.0 %collective-permute-start.3 = (bf16[128,2048]{1,0:T(8,128)(2,1)}, bf16[128,2048]{1,0:T(8,128)(2,1)S(1)}, u32[]{:S(2)}, u32[]{:S(2)}) collective-permute-start(bf16[128,2048]{1,0:T(8,128)(2,1)} %refs_0_.1), channel_id=1, source_target_pairs={{0,4},{4,8},{8,12},{12,14},{14,10},{10,6},{6,2},{2,0},{1,5},{5,9},... | collective-permute-start | bytes 1572872 | tf_op jit(solution)/shard_map/ppermute | solution.py:297
  3.7 15.1 %collective-permute-start.4 = (bf16[128,2048]{1,0:T(8,128)(2,1)}, bf16[128,2048]{1,0:T(8,128)(2,1)S(1)}, u32[]{:S(2)}, u32[]{:S(2)}) collective-permute-start(bf16[128,2048]{1,0:T(8,128)(2,1)} %refs_0_.1), channel_id=1, source_target_pairs={{4,0},{8,4},{12,8},{14,12},{10,14},{6,10},{2,6},{0,2},{5,1},{9,5},... | collective-permute-start | bytes 1572872 | tf_op jit(solution)/shard_map/ppermute | solution.py:297
  3.7 23.3 %collective-permute-start.5 = (bf16[128,2048]{1,0:T(8,128)(2,1)}, bf16[128,2048]{1,0:T(8,128)(2,1)S(1)}, u32[]{:S(2)}, u32[]{:S(2)}) collective-permute-start(bf16[128,2048]{1,0:T(8,128)(2,1)} %refs_1_.1), channel_id=1, source_target_pairs={{0,4},{4,8},{8,12},{12,14},{14,10},{10,6},{6,2},{2,0},{1,5},{5,9},... | collective-permute-start | bytes 1572872 | tf_op jit(solution)/shard_map/ppermute | solution.py:297
  5.7 23.1 %collective-permute-start.6 = (bf16[128,2048]{1,0:T(8,128)(2,1)}, bf16[128,2048]{1,0:T(8,128)(2,1)S(1)}, u32[]{:S(2)}, u32[]{:S(2)}) collective-permute-start(bf16[128,2048]{1,0:T(8,128)(2,1)} %refs_1_.1), channel_id=1, source_target_pairs={{4,0},{8,4},{12,8},{14,12},{10,14},{6,10},{2,6},{0,2},{5,1},{9,5},... | collective-permute-start | bytes 1572872 | tf_op jit(solution)/shard_map/ppermute | solution.py:297
  5.7 113.5 %collective-permute-start = (bf16[2,2048,384]{2,1,0:T(8,128)(2,1)}, bf16[2,2048,384]{2,1,0:T(8,128)(2,1)}, u32[]{:S(2)}, u32[]{:S(2)}) collective-permute-start(bf16[2,2048,384]{2,1,0:T(8,128)(2,1)} %refs_5_.9), channel_id=1, source_target_pairs={{0,1},{1,0},{2,3},{3,2},{4,5},{5,4},{6,7},{7,6},{8,9},{9,8},{10,11... | collective-permute-start | bytes 9437192 | tf_op jit(solution)/shard_map/ppermute | solution.py:301
  16.6 102.6 %collective-permute-start.1 = (bf16[2,2048,384]{2,1,0:T(8,128)(2,1)}, bf16[2,2048,384]{2,1,0:T(8,128)(2,1)}, u32[]{:S(2)}, u32[]{:S(2)}) collective-permute-start(bf16[2,2048,384]{2,1,0:T(8,128)(2,1)} %refs_6_.7), channel_id=1, source_target_pairs={{0,1},{1,0},{2,3},{3,2},{4,5},{5,4},{6,7},{7,6},{8,9},{9,8},{10,11... | collective-permute-start | bytes 9437192 | tf_op jit(solution)/shard_map/ppermute | solution.py:301
  18.8 100.5 %collective-permute-start.2 = (bf16[2,384,2048]{2,1,0:T(8,128)(2,1)}, bf16[2,384,2048]{2,1,0:T(8,128)(2,1)}, u32[]{:S(2)}, u32[]{:S(2)}) collective-permute-start(bf16[2,384,2048]{2,1,0:T(8,128)(2,1)} %refs_7_.7), channel_id=1, source_target_pairs={{0,1},{1,0},{2,3},{3,2},{4,5},{5,4},{6,7},{7,6},{8,9},{9,8},{10,11... | collective-permute-start | bytes 9437192 | tf_op jit(solution)/shard_map/ppermute | solution.py:301
  27.0 13.1 %collective-permute-start.7 = (bf16[128,2048]{1,0:T(8,128)(2,1)S(1)}, bf16[128,2048]{1,0:T(8,128)(2,1)S(1)}, u32[]{:S(2)}, u32[]{:S(2)}) collective-permute-start(bf16[128,2048]{1,0:T(8,128)(2,1)S(1)} %collective-permute-done.3.refs_0_), channel_id=1, source_target_pairs={{0,4},{4,8},{8,12},{12,14},{14,10},{10,6},{6,2},{2,0},{1,5},{5,9},... | collective-permute-start | bytes 1572872 | tf_op jit(solution)/shard_map/ppermute | solution.py:297
  28.8 13.6 %collective-permute-start.8 = (bf16[128,2048]{1,0:T(8,128)(2,1)S(1)}, bf16[128,2048]{1,0:T(8,128)(2,1)S(1)}, u32[]{:S(2)}, u32[]{:S(2)}) collective-permute-start(bf16[128,2048]{1,0:T(8,128)(2,1)S(1)} %collective-permute-done.4.refs_1_), channel_id=1, source_target_pairs={{4,0},{8,4},{12,8},{14,12},{10,14},{6,10},{2,6},{0,2},{5,1},{9,5},... | collective-permute-start | bytes 1572872 | tf_op jit(solution)/shard_map/ppermute | solution.py:297
  40.1 12.3 %collective-permute-start.9 = (bf16[128,2048]{1,0:T(8,128)(2,1)S(1)}, bf16[128,2048]{1,0:T(8,128)(2,1)}, u32[]{:S(2)}, u32[]{:S(2)}) collective-permute-start(bf16[128,2048]{1,0:T(8,128)(2,1)S(1)} %collective-permute-done.5.refs_2_), channel_id=1, source_target_pairs={{0,4},{4,8},{8,12},{12,14},{14,10},{10,6},{6,2},{2,0},{1,5},{5,9},... | collective-permute-start | bytes 1572872 | tf_op jit(solution)/shard_map/ppermute | solution.py:297
  41.6 0.8 copy-start.5
  42.4 12.1 %collective-permute-start.10 = (bf16[128,2048]{1,0:T(8,128)(2,1)S(1)}, bf16[128,2048]{1,0:T(8,128)(2,1)}, u32[]{:S(2)}, u32[]{:S(2)}) collective-permute-start(bf16[128,2048]{1,0:T(8,128)(2,1)S(1)} %collective-permute-done.6.refs_3_), channel_id=1, source_target_pairs={{4,0},{8,4},{12,8},{14,12},{10,14},{6,10},{2,6},{0,2},{5,1},{9,5},... | collective-permute-start | bytes 1572872 | tf_op jit(solution)/shard_map/ppermute | solution.py:297
  43.0 0.8 copy-start.7
  52.4 11.9 %collective-permute-start.11 = (bf16[128,2048]{1,0:T(8,128)(2,1)S(1)}, bf16[128,2048]{1,0:T(8,128)(2,1)S(1)}, u32[]{:S(2)}, u32[]{:S(2)}) collective-permute-start(bf16[128,2048]{1,0:T(8,128)(2,1)S(1)} %collective-permute-done.7.refs_0_), channel_id=1, source_target_pairs={{0,4},{4,8},{8,12},{12,14},{14,10},{10,6},{6,2},{2,0},{1,5},{5,9},... | collective-permute-start | bytes 1572872 | tf_op jit(solution)/shard_map/ppermute | solution.py:297
  53.7 0.8 copy-start.9
  54.5 11.9 %collective-permute-start.12 = (bf16[128,2048]{1,0:T(8,128)(2,1)S(1)}, bf16[128,2048]{1,0:T(8,128)(2,1)S(1)}, u32[]{:S(2)}, u32[]{:S(2)}) collective-permute-start(bf16[128,2048]{1,0:T(8,128)(2,1)S(1)} %collective-permute-done.8.refs_1_), channel_id=1, source_target_pairs={{4,0},{8,4},{12,8},{14,12},{10,14},{6,10},{2,6},{0,2},{5,1},{9,5},... | collective-permute-start | bytes 1572872 | tf_op jit(solution)/shard_map/ppermute | solution.py:297
  55.2 0.8 copy-start.11
  64.3 15.0 %collective-permute-start.13 = (bf16[128,2048]{1,0:T(8,128)(2,1)}, bf16[128,2048]{1,0:T(8,128)(2,1)S(1)}, u32[]{:S(2)}, u32[]{:S(2)}) collective-permute-start(bf16[128,2048]{1,0:T(8,128)(2,1)} %collective-permute-done.9.refs_2_), channel_id=1, source_target_pairs={{0,4},{4,8},{8,12},{12,14},{14,10},{10,6},{6,2},{2,0},{1,5},{5,9},... | collective-permute-start | bytes 1572872 | tf_op jit(solution)/shard_map/ppermute | solution.py:297
  66.4 14.3 %collective-permute-start.14 = (bf16[128,2048]{1,0:T(8,128)(2,1)}, bf16[128,2048]{1,0:T(8,128)(2,1)S(1)}, u32[]{:S(2)}, u32[]{:S(2)}) collective-permute-start(bf16[128,2048]{1,0:T(8,128)(2,1)} %collective-permute-done.10.refs_3_), channel_id=1, source_target_pairs={{4,0},{8,4},{12,8},{14,12},{10,14},{6,10},{2,6},{0,2},{5,1},{9,5},... | collective-permute-start | bytes 1572872 | tf_op jit(solution)/shard_map/ppermute | solution.py:297
  79.3 33.4 %collective-permute-start.15 = (bf16[64,2048]{1,0:T(8,128)(2,1)S(1)}, bf16[64,2048]{1,0:T(8,128)(2,1)S(1)}, u32[]{:S(2)}, u32[]{:S(2)}) collective-permute-start(bf16[64,2048]{1,0:T(8,128)(2,1)S(1)} %slice.74), channel_id=1, source_target_pairs={{0,4},{4,8},{8,12},{12,14},{14,10},{10,6},{6,2},{2,0},{1,5},{5,9},... | collective-permute-start | bytes 786440 | tf_op jit(solution)/shard_map/ppermute | solution.py:297
  80.6 32.2 %collective-permute-start.16 = (bf16[64,2048]{1,0:T(8,128)(2,1)S(1)}, bf16[64,2048]{1,0:T(8,128)(2,1)S(1)}, u32[]{:S(2)}, u32[]{:S(2)}) collective-permute-start(bf16[64,2048]{1,0:T(8,128)(2,1)S(1)} %slice.75), channel_id=1, source_target_pairs={{4,0},{8,4},{12,8},{14,12},{10,14},{6,10},{2,6},{0,2},{5,1},{9,5},... | collective-permute-start | bytes 786440 | tf_op jit(solution)/shard_map/ppermute | solution.py:297
  112.7 6.4 %collective-permute-start.17 = (bf16[64,2048]{1,0:T(8,128)(2,1)S(1)}, bf16[64,2048]{1,0:T(8,128)(2,1)S(1)}, u32[]{:S(2)}, u32[]{:S(2)}) collective-permute-start(bf16[64,2048]{1,0:T(8,128)(2,1)S(1)} %slice.76), channel_id=1, source_target_pairs={{0,4},{4,8},{8,12},{12,14},{14,10},{10,6},{6,2},{2,0},{1,5},{5,9},... | collective-permute-start | bytes 786440 | tf_op jit(solution)/shard_map/ppermute | solution.py:297
  112.8 6.4 %collective-permute-start.18 = (bf16[64,2048]{1,0:T(8,128)(2,1)S(1)}, bf16[64,2048]{1,0:T(8,128)(2,1)S(1)}, u32[]{:S(2)}, u32[]{:S(2)}) collective-permute-start(bf16[64,2048]{1,0:T(8,128)(2,1)S(1)} %slice.77), channel_id=1, source_target_pairs={{4,0},{8,4},{12,8},{14,12},{10,14},{6,10},{2,6},{0,2},{5,1},{9,5},... | collective-permute-start | bytes 786440 | tf_op jit(solution)/shard_map/ppermute | solution.py:297
  119.3 1.9 copy-start
  121.1 1.9 copy-start.2
  123.0 13.4 %copy-start.1 = (bf16[2,2048,384]{2,1,0:T(8,128)(2,1)S(1)}, bf16[2,2048,384]{2,1,0:T(8,128)(2,1)}, u32[]{:S(2)}) copy-start(bf16[2,2048,384]{2,1,0:T(8,128)(2,1)} %refs_5_.9) | copy-start | bytes 9437188
  134.4 16.7 %collective-permute-start.19 = (bf16[64,2176]{1,0:T(8,128)(2,1)S(1)}, bf16[64,2176]{1,0:T(8,128)(2,1)S(1)}, u32[]{:S(2)}, u32[]{:S(2)}) collective-permute-start(bf16[64,2176]{1,0:T(8,128)(2,1)S(1)} %get-tuple-element.16), channel_id=1, source_target_pairs={{4,0},{8,4},{12,8},{14,12},{10,14},{6,10},{2,6},{0,2},{5,1},{9,5},... | collective-permute-start | bytes 835592 | tf_op jit(solution)/shard_map/ppermute | solution.py:297
  136.4 14.7 %collective-permute-start.23 = (bf16[64,2176]{1,0:T(8,128)(2,1)S(1)}, bf16[64,2176]{1,0:T(8,128)(2,1)S(1)}, u32[]{:S(2)}, u32[]{:S(2)}) collective-permute-start(bf16[64,2176]{1,0:T(8,128)(2,1)S(1)} %get-tuple-element.17), channel_id=1, source_target_pairs={{0,4},{4,8},{8,12},{12,14},{14,10},{10,6},{6,2},{2,0},{1,5},{5,9},... | collective-permute-start | bytes 835592 | tf_op jit(solution)/shard_map/ppermute | solution.py:297
  151.2 2.4 %copy-start.10 = (bf16[128,2048]{1,0:T(8,128)(2,1)S(1)}, bf16[128,2048]{1,0:T(8,128)(2,1)}, u32[]{:S(2)}) copy-start(bf16[128,2048]{1,0:T(8,128)(2,1)} %copy-done.9) | copy-start | bytes 1572868
  151.2 2.4 %copy-start.12 = (bf16[128,2048]{1,0:T(8,128)(2,1)S(1)}, bf16[128,2048]{1,0:T(8,128)(2,1)}, u32[]{:S(2)}) copy-start(bf16[128,2048]{1,0:T(8,128)(2,1)} %copy-done.11) | copy-start | bytes 1572868
  151.3 17.0 %collective-permute-start.24 = (bf16[128,2176]{1,0:T(8,128)(2,1)S(1)}, bf16[128,2176]{1,0:T(8,128)(2,1)S(1)}, u32[]{:S(2)}, u32[]{:S(2)}) collective-permute-start(bf16[128,2176]{1,0:T(8,128)(2,1)S(1)} %pad_maximum_fusion.1), channel_id=1, source_target_pairs={{0,4},{4,8},{8,12},{12,14},{14,10},{10,6},{6,2},{2,0},{1,5},{5,9},... | collective-permute-start | bytes 1671176 | tf_op jit(solution)/shard_map/ppermute | solution.py:297
  153.3 14.9 %collective-permute-start.20 = (bf16[128,2176]{1,0:T(8,128)(2,1)S(1)}, bf16[128,2176]{1,0:T(8,128)(2,1)S(1)}, u32[]{:S(2)}, u32[]{:S(2)}) collective-permute-start(bf16[128,2176]{1,0:T(8,128)(2,1)S(1)} %pad_maximum_fusion), channel_id=1, source_target_pairs={{4,0},{8,4},{12,8},{14,12},{10,14},{6,10},{2,6},{0,2},{5,1},{9,5},... | collective-permute-start | bytes 1671176 | tf_op jit(solution)/shard_map/ppermute | solution.py:297
  168.2 3.2 %copy-start.6 = (bf16[128,2048]{1,0:T(8,128)(2,1)S(1)}, bf16[128,2048]{1,0:T(8,128)(2,1)}, u32[]{:S(2)}) copy-start(bf16[128,2048]{1,0:T(8,128)(2,1)} %copy-done.5) | copy-start | bytes 1572868
  168.2 3.2 %copy-start.8 = (bf16[128,2048]{1,0:T(8,128)(2,1)S(1)}, bf16[128,2048]{1,0:T(8,128)(2,1)}, u32[]{:S(2)}) copy-start(bf16[128,2048]{1,0:T(8,128)(2,1)} %copy-done.7) | copy-start | bytes 1572868
  168.5 17.5 %collective-permute-start.21 = (bf16[128,2176]{1,0:T(8,128)(2,1)S(1)}, bf16[128,2176]{1,0:T(8,128)(2,1)S(1)}, u32[]{:S(2)}, u32[]{:S(2)}) collective-permute-start(bf16[128,2176]{1,0:T(8,128)(2,1)S(1)} %get-tuple-element.10), channel_id=1, source_target_pairs={{4,0},{8,4},{12,8},{14,12},{10,14},{6,10},{2,6},{0,2},{5,1},{9,5},... | collective-permute-start | bytes 1671176 | tf_op jit(solution)/shard_map/ppermute | solution.py:297
  170.5 15.5 %collective-permute-start.25 = (bf16[128,2176]{1,0:T(8,128)(2,1)S(1)}, bf16[128,2176]{1,0:T(8,128)(2,1)S(1)}, u32[]{:S(2)}, u32[]{:S(2)}) collective-permute-start(bf16[128,2176]{1,0:T(8,128)(2,1)S(1)} %get-tuple-element.11), channel_id=1, source_target_pairs={{0,4},{4,8},{8,12},{12,14},{14,10},{10,6},{6,2},{2,0},{1,5},{5,9},... | collective-permute-start | bytes 1671176 | tf_op jit(solution)/shard_map/ppermute | solution.py:297
  186.0 3.1 %copy-start.3 = (bf16[128,2048]{1,0:T(8,128)(2,1)S(1)}, bf16[128,2048]{1,0:T(8,128)(2,1)}, u32[]{:S(2)}) copy-start(bf16[128,2048]{1,0:T(8,128)(2,1)} %refs_0_.1) | copy-start | bytes 1572868
  186.0 3.1 %copy-start.4 = (bf16[128,2048]{1,0:T(8,128)(2,1)S(1)}, bf16[128,2048]{1,0:T(8,128)(2,1)}, u32[]{:S(2)}) copy-start(bf16[128,2048]{1,0:T(8,128)(2,1)} %refs_1_.1) | copy-start | bytes 1572868
  186.3 14.0 %collective-permute-start.22 = (bf16[128,2176]{1,0:T(8,128)(2,1)S(1)}, bf16[128,2176]{1,0:T(8,128)(2,1)S(1)}, u32[]{:S(2)}, u32[]{:S(2)}) collective-permute-start(bf16[128,2176]{1,0:T(8,128)(2,1)S(1)} %get-tuple-element.8), channel_id=1, source_target_pairs={{4,0},{8,4},{12,8},{14,12},{10,14},{6,10},{2,6},{0,2},{5,1},{9,5},... | collective-permute-start | bytes 1671176 | tf_op jit(solution)/shard_map/ppermute | solution.py:297
  187.6 12.7 %collective-permute-start.26 = (bf16[128,2176]{1,0:T(8,128)(2,1)S(1)}, bf16[128,2176]{1,0:T(8,128)(2,1)S(1)}, u32[]{:S(2)}, u32[]{:S(2)}) collective-permute-start(bf16[128,2176]{1,0:T(8,128)(2,1)S(1)} %get-tuple-element.9), channel_id=1, source_target_pairs={{0,4},{4,8},{8,12},{12,14},{14,10},{10,6},{6,2},{2,0},{1,5},{5,9},... | collective-permute-start | bytes 1671176 | tf_op jit(solution)/shard_map/ppermute | solution.py:297
